TPU v7x, 128 devices: a whole 4x4x4 slice. The times are simulated.
128 devices in a mesh: dp: 16 (over x, y), red: 8 (over z, core).
Axes of the slice: x: 4, y: 4, z: 4, core: 2. Of those that a mesh axis runs over, the one named last changes fastest.
Arguments:
- frames: bfloat16 [2048, 48, 1536], P(('dp', 'red')), may hold values from -36 to 36
- cotangent: bfloat16 [2048, 48, 1536], P(('dp', 'red')), may hold values from -6 to 6
- w_in: bfloat16 [1536, 3072], P('red'), may hold values from -0.15625 to 0.15625
- kernel: float32 [31, 1536], replicated, may hold values from -1 to 1
- gain: float32 [1536], replicated, may hold values from 0.25 to 1.75
- lengths: int32 [2048], replicated, may hold values from 1 to 47, as said below
Outputs:
- module_output: bfloat16 [2048, 48, 1536], P(('dp', 'red'))
- frame_gradient: bfloat16 [2048, 48, 1536], P(('dp', 'red'))
- grad_w_in: float32 [1536, 3072], P('red')
- grad_kernel: float32 [31, 1536], replicated
- grad_gain: float32 [1536], replicated
Inputs may be any that keep to these rules, and one draw needn't show every extreme that they name: The slots of each device, in order, form 16 groups of 1 slots. The q-th slot of group j on the device with dp index i and red index r and the q-th slot of group j on the device with dp index (2 j + 1 - i) mod 16 and the same red index have lengths that sum to exactly 48. The slots of dp index 0 all hold at least three quarters of 48 frames, rounded up.
All inputs are finite; a program needn't handle non-finite values.
Results may differ from a plain program's by a relative error of at most 0.0054.
Values may be sent and summed in bfloat16 or wider, within the bound.
A program may use at most 128 MiB of HBM per device.

v0:
```python
import jax
import jax.numpy as jnp
from jax import lax
from jax.sharding import PartitionSpec as P

EPSILON = 1e-05


def normalize(widened_frames):
    center = widened_frames - jnp.mean(widened_frames, axis=-1, keepdims=True)
    inv_std = lax.rsqrt(jnp.mean(center * center, axis=-1, keepdims=True) + EPSILON)
    return (center * inv_std, inv_std)


def block_pass(frames, cotangent, valid_frame_mask, segment, weights, kernel, gain):
    row_count, length, model_width = frames.shape
    tap_count = kernel.shape[0]
    reach = tap_count // 2
    widened_frames = frames.astype(jnp.float32)
    normed, inv_std = normalize(widened_frames)
    scaled = (normed * gain).astype(jnp.bfloat16)
    flat_in = scaled.reshape(row_count * length, model_width)
    hidden = jnp.dot(flat_in, weights, preferred_element_type=jnp.float32)
    hidden = hidden.reshape(row_count, length, 2 * model_width)
    value_portion = hidden[..., :model_width]
    gate_sigmoid = jax.nn.sigmoid(hidden[..., model_width:])
    frame_validity = valid_frame_mask.astype(jnp.float32)[..., None]
    gated_linear_output = value_portion * gate_sigmoid * frame_validity
    padded = jnp.pad(gated_linear_output, ((0, 0), (reach, reach), (0, 0)))
    seg_pad = jnp.pad(segment, ((0, 0), (reach, reach)), constant_values=-1)
    convolved_frames = jnp.zeros_like(gated_linear_output)
    for offset in range(tap_count):
        window = padded[:, offset : offset + length]
        same_seg = (seg_pad[:, offset : offset + length] == segment).astype(jnp.float32)[..., None]
        convolved_frames = convolved_frames + kernel[offset] * (window * same_seg)
    swish_activation = jax.nn.sigmoid(convolved_frames)
    module_output = (
        (widened_frames + convolved_frames * swish_activation) * frame_validity
    ).astype(jnp.bfloat16)
    incoming_gradient = cotangent.astype(jnp.float32) * frame_validity
    grad_conv = incoming_gradient * (
        swish_activation * (1.0 + convolved_frames * (1.0 - swish_activation))
    )
    grad_pad = jnp.pad(grad_conv, ((0, 0), (reach, reach), (0, 0)))
    gated_linear_gradient = jnp.zeros_like(gated_linear_output)
    kernel_terms = []
    for offset in range(tap_count):
        window = padded[:, offset : offset + length]
        same_seg = (seg_pad[:, offset : offset + length] == segment).astype(jnp.float32)[..., None]
        kernel_terms.append(jnp.sum(grad_conv * window * same_seg, axis=(0, 1)))
        back_start = 2 * reach - offset
        back_same = (seg_pad[:, back_start : back_start + length] == segment).astype(jnp.float32)[
            ..., None
        ]
        gated_linear_gradient = gated_linear_gradient + kernel[offset] * (
            grad_pad[:, back_start : back_start + length] * back_same
        )
    gated_linear_gradient = gated_linear_gradient * frame_validity
    grad_hidden = jnp.concatenate(
        [
            gated_linear_gradient * gate_sigmoid,
            gated_linear_gradient * value_portion * gate_sigmoid * (1.0 - gate_sigmoid),
        ],
        axis=-1,
    ).astype(jnp.bfloat16)
    flat_grad = grad_hidden.reshape(row_count * length, 2 * model_width)
    grad_scaled = lax.dot_general(
        flat_grad, weights, (((1,), (1,)), ((), ())), preferred_element_type=jnp.float32
    )
    grad_scaled = grad_scaled.reshape(row_count, length, model_width)
    gain_term = jnp.sum(grad_scaled * normed, axis=(0, 1))
    grad_normed = grad_scaled * gain
    frame_gradient = incoming_gradient + inv_std * (
        grad_normed
        - jnp.mean(grad_normed, axis=-1, keepdims=True)
        - normed * jnp.mean(grad_normed * normed, axis=-1, keepdims=True)
    )
    frame_gradient = (frame_gradient * frame_validity).astype(jnp.bfloat16)
    return (module_output, frame_gradient, flat_in, flat_grad, jnp.stack(kernel_terms), gain_term)


def local(frames, cotangent, w_in, kernel, gain, lengths):
    dp_size = lax.axis_size("dp")
    red_size = lax.axis_size("red")
    dp_index = lax.axis_index("dp")
    red_index = lax.axis_index("red")
    local_utts, length, model_width = frames.shape
    weights = lax.all_gather(w_in, "red", axis=0, tiled=True)
    positions = jnp.arange(length, dtype=jnp.int32)
    by_owner = lengths.reshape(dp_size, red_size, local_utts)
    own_lengths = lax.dynamic_slice(by_owner, (dp_index, red_index, 0), (1, 1, local_utts)).reshape(
        local_utts
    )
    valid_frame_mask = positions[None, :] < own_lengths[:, None]
    segment = jnp.where(valid_frame_mask, 0, 1).astype(jnp.int32)
    module_output, frame_gradient, flat_in, flat_grad, kernel_part, gain_part = block_pass(
        frames, cotangent, valid_frame_mask, segment, weights, kernel, gain
    )
    grad_scale = lax.rsqrt(jnp.sum(lengths).astype(jnp.float32))
    block_rows = model_width // (dp_size * red_size)
    ordered = flat_in.reshape(-1, red_size, dp_size, block_rows)
    ordered = jnp.transpose(ordered, (0, 2, 1, 3)).reshape(-1, model_width)
    owned_rows = lax.psum_scatter(
        lax.dot_general(
            ordered, flat_grad, (((0,), (0,)), ((), ())), preferred_element_type=jnp.float32
        ),
        ("dp", "red"),
        scatter_dimension=0,
        tiled=True,
    )
    grad_weights = lax.all_gather(owned_rows, "dp", axis=0, tiled=True)
    kernel_total, gain_total = lax.psum((kernel_part, gain_part), ("dp", "red"))
    return (
        module_output,
        frame_gradient,
        grad_weights * grad_scale,
        kernel_total * grad_scale,
        gain_total * grad_scale,
    )


def solution(mesh):
    placed = (
        P(("dp", "red"), None, None),
        P(("dp", "red"), None, None),
        P("red", None),
        P(),
        P(),
        P(),
    )
    return jax.shard_map(
        local,
        mesh=mesh,
        in_specs=placed,
        out_specs=(
            P(("dp", "red"), None, None),
            P(("dp", "red"), None, None),
            P("red", None),
            P(),
            P(),
        ),
        check_vma=False,
    )
```

profile of v0, /device:TPU:1, one launch (start us, length us, event | category | flops | bytes accessed | tf_op | source)
XLA Modules:
  0.0 923.5 jit_solution(477016552205187638)
XLA Ops:
  14.4 8.3 copy.13
  22.7 10.7 %reshape_reshape.3 = bf16[768,8,16,12]{0,3,2,1:T(8,128)(2,1)} reshape(bf16[16,48,1536]{1,0,2:T(8,128)(2,1)} %copy.13) | data formatting | bytes 4718592 | tf_op jit(solution)/shard_map/reshape;reshape | solution.py:101
  33.4 4.0 copy.14
  37.4 5.2 reshape.139
  43.8 23.9 %all-gather.4.cloned.1.call-done = bf16[1536,3072]{1,0:T(8,128)(2,1)} async-done(((bf16[192,3072]{1,0:T(8,128)(2,1)}), bf16[1536,3072]{1,0:T(8,128)(2,1)}) %all-gather.4.cloned.1.call-update) | async-done | bytes 9437200 | tf_op jit(solution)/shard_map/all_gather | solution.py:88
  67.7 10.8 %fusion.3 = f32[16,48,3072]{2,1,0:T(8,128)S(1)} fusion(bf16[16,48,1536]{2,1,0:T(8,128)(2,1)} %fusion.11, bf16[1536,3072]{1,0:T(8,128)(2,1)} %all-gather.4.cloned.1.call-done), kind=kOutput, calls=%fused_computation.62 | convolution fusion | flops 7247757312 | bytes 21233664 | tf_op jit(solution)/shard_map/dot_general | solution.py:23
  82.6 49.2 %multiply_reduce_fusion = (f32[1536]{0:T(1024)}, f32[1536]{0:T(1024)}, f32[1536]{0:T(1024)}, f32[1536]{0:T(1024)}, f32[1536]{0:T(1024)}, /*index=5*/f32[1536]{0:...) fusion(f32[16,48,1536]{2,1,0:T(8,128)S(1)} %multiply_multiply_f, ...), kind=kLoop, calls=%fused_computation.186 | loop fusion | flops 150981120 | bytes 16856064 | tf_op jit(solution)/shard_map/reduce_sum | solution.py:50
  132.0 28.6 %multiply_convert_fusion.1 = (bf16[16,48,1536]{2,1,0:T(8,128)(2,1)S(1)}, f32[16,48,1536]{2,1,0:T(8,128)}) fusion(f32[16,48,3072]{2,1,0:T(8,128)} %copy-done.3, f32[16,48]{1,0:T(8,128)S(1)} %get-tuple-element.106, f32[16,48]{1,0:T(8,128)S(1)} %get-tuple-element.76, f32[1536]{0:T(1024)} %copy-done.57, f32[16,48]{1,0:T(8,128)S(1)} %get-tuple-element.77, ...), kind=kLoop, calls=%fused_computation.218 | loop fusion | flops 114425856 | bytes 16800768 | tf_op jit(solution)/shard_map/convert.4
  160.6 6.9 multiply_convert_fusion
  168.9 10.8 %fusion.119 = f32[1536,3072]{1,0:T(8,128)} fusion(bf16[768,1536]{0,1:T(8,128)(2,1)S(1)} %copy-done.8, bf16[768,1536]{1,0:T(8,128)(2,1)S(1)} %bitcast.24, bf16[768,1536]{1,0:T(8,128)(2,1)S(1)} %bitcast.23), kind=kOutput, calls=%fused_computation.182 | convolution fusion | flops 7257194496 | bytes 25952256 | tf_op jit(solution)/shard_map/dot_general | solution.py:104
  179.8 359.8 %fusion = f32[16,3072]{1,0:T(8,128)S(1)} fusion(f32[1536,3072]{1,0:T(8,128)} %fusion.119), kind=kCustom, calls=%all-reduce-scatter | all-reduce-scatter fusion | flops 6291457 | bytes 19070976
  552.0 15.3 %collective-permute-start.22 = (f32[16,3072]{1,0:T(8,128)S(1)}, f32[16,3072]{1,0:T(8,128)S(1)}, u32[]{:S(2)}, u32[]{:S(2)}) collective-permute-start(f32[16,3072]{1,0:T(8,128)S(1)} %fusion), channel_id=1, source_target_pairs={{0,23},{1,24},{2,25},{3,26},{4,27},{5,28},{6,29},{7,30},{8,31},{9,... | collective-permute-start | bytes 589832
  567.3 6.4 collective-permute-start.21
  573.7 5.7 collective-permute-start.20
  579.4 8.4 collective-permute-start.19
  589.8 5.9 collective-permute-start.17
  603.1 5.5 collective-permute-start.14
  608.6 12.3 %collective-permute-start.13 = (f32[16,3072]{1,0:T(8,128)S(1)}, f32[16,3072]{1,0:T(8,128)S(1)}, u32[]{:S(2)}, u32[]{:S(2)}) collective-permute-start(f32[16,3072]{1,0:T(8,128)S(1)} %fusion), channel_id=1, source_target_pairs={{0,14},{1,15},{2,16},{3,17},{4,18},{5,19},{6,20},{7,21},{8,22},{9,... | collective-permute-start | bytes 589832
  620.9 10.3 %collective-permute-start.12 = (f32[16,3072]{1,0:T(8,128)S(1)}, f32[16,3072]{1,0:T(8,128)S(1)}, u32[]{:S(2)}, u32[]{:S(2)}) collective-permute-start(f32[16,3072]{1,0:T(8,128)S(1)} %fusion), channel_id=1, source_target_pairs={{0,13},{1,14},{2,15},{3,16},{4,17},{5,18},{6,19},{7,20},{8,21},{9,... | collective-permute-start | bytes 589832
  631.2 14.7 %collective-permute-start.11 = (f32[16,3072]{1,0:T(8,128)S(1)}, f32[16,3072]{1,0:T(8,128)S(1)}, u32[]{:S(2)}, u32[]{:S(2)}) collective-permute-start(f32[16,3072]{1,0:T(8,128)S(1)} %fusion), channel_id=1, source_target_pairs={{0,12},{1,13},{2,14},{3,15},{4,16},{5,17},{6,18},{7,19},{8,20},{9,... | collective-permute-start | bytes 589832
  647.3 26.0 %multiply_reduce_fusion.9 = (f32[1536]{0:T(1024)S(1)}, f32[1536]{0:T(1024)S(1)}, f32[1536]{0:T(1024)S(1)}, f32[1536]{0:T(1024)S(1)}, f32[1536]{0:T(1024)S(1)}, /...) fusion(f32[16,48,1536]{2,1,0:T(8,128)} %copy-done.1, f32[16,48,1536]{2,1,0:T(8,128)} %copy-done, ...), kind=kLoop, calls=%fused_computation.195 | loop fusion | flops 30657024 | bytes 9517056 | tf_op jit(solution)/shard_map/reduce_sum | solution.py:50
  674.6 5.2 collective-permute-start.8
  687.9 9.0 multiply_reduce_fusion.18
  697.0 6.7 collective-permute-start.4
  705.7 4.6 collective-permute-start.2
  715.0 3.9 multiply_reduce_fusion.27
  722.4 84.8 %concatenate.17 = f32[524,3072]{1,0:T(8,128)} concatenate(f32[12,3072]{1,0:T(8,128)S(1)} %collective-permute-done.31, f32[16,3072]{1,0:T(8,128)S(1)} %collective-permute-done.30, f32[16,3072]{1,0:T(8,128)} %copy-done.9, f32[16,3072]{1,0:T(8,128)} %copy-done.10, f32[16,3072]{1,0:T(8,128)} %copy-done.11, f32[16,3072]{1,0:T(8,128)} %copy-done.12, f32[16,3072]{1,0:T(8,128)} %copy-done.13, ...), dimensions={0} | concatenate | bytes 12877824
  808.9 14.3 %fusion.18 = (f32[1536]{0:T(1024)S(1)}, f32[16,48]{1,0:T(8,128)S(1)}, f32[16,48]{1,0:T(8,128)S(1)}, f32[16,48,1536]{2,1,0:T(8,128)}) fusion(bf16[16,48,1536]{2,1,0:T(8,128)(2,1)S(1)} %copy-done.4, f32[16,48]{1,0:T(8,128)S(1)} %copy-done.60, f32[16,48]{1,0:T(8,128)S(1)} %copy-done.52, f32[1536]{0:T(1024)S(1)} %copy-done.62, ...), kind=kOutput, calls=%fused_computation.80 | convolution fusion | flops 7267808256 | bytes 21258240 | tf_op jit(solution)/shard_map/dot_general | solution.py:67
  823.2 63.9 %psum.15 = f32[1536]{0:T(1024)S(1)} all-reduce(f32[1536]{0:T(1024)S(1)} %get-tuple-element.36), channel_id=1, replica_groups=mesh['dp'=16,'red'=8] {'dp','red'}, use_global_device_ids=true, to_apply=%region_39.40 | all-reduce | flops 1536 | bytes 12288 | tf_op jit(solution)/shard_map/psum | solution.py:112
  887.7 7.8 fusion.17
  897.2 12.9 %all-gather.6.cloned.1.call-done = f32[16,12,3072]{2,1,0:T(8,128)} async-done(((f32[1,12,3072]{2,1,0:T(8,128)}), f32[16,12,3072]{2,1,0:T(8,128)}) %all-gather.6.cloned.1.call-update) | async-done | bytes 2359312 | tf_op jit(solution)/shard_map/all_gather | solution.py:111
  910.1 3.9 broadcast_multiply_fusion
  (264 shorter events, 61.6 us)
Async XLA Ops:
  7.2 60.5 %all-gather.4.cloned.1.call-start = ((), (), s32[]{:S(2)}) async-start(), calls=%async_computation | async-start | bytes 10616832 | tf_op jit(solution)/shard_map/all_gather | solution.py:88
  7.9 887.6 %all-reduce.7.cloned.1.call-start = ((), (), s32[]{:S(2)}) async-start(), calls=%async_computation.1 | async-start | bytes 393216 | tf_op jit(solution)/shard_map/psum | solution.py:112
  539.6 7.9 collective-permute-start.30
  544.9 7.2 collective-permute-start.27
  546.2 21.1 %collective-permute-start.26 = (f32[16,3072]{1,0:T(8,128)S(1)}, f32[16,3072]{1,0:T(8,128)S(1)}, u32[]{:S(2)}, u32[]{:S(2)}) collective-permute-start(f32[16,3072]{1,0:T(8,128)S(1)} %fusion), channel_id=1, source_target_pairs={{0,27},{1,28},{2,29},{3,30},{4,31},{5,32},{6,33},{7,34},{8,35},{9,... | collective-permute-start | bytes 589832
  547.5 26.2 %collective-permute-start.25 = (f32[16,3072]{1,0:T(8,128)S(1)}, f32[16,3072]{1,0:T(8,128)S(1)}, u32[]{:S(2)}, u32[]{:S(2)}) collective-permute-start(f32[16,3072]{1,0:T(8,128)S(1)} %fusion), channel_id=1, source_target_pairs={{0,26},{1,27},{2,28},{3,29},{4,30},{5,31},{6,32},{7,33},{8,34},{9,... | collective-permute-start | bytes 589832
  548.8 30.6 %collective-permute-start.24 = (f32[16,3072]{1,0:T(8,128)S(1)}, f32[16,3072]{1,0:T(8,128)S(1)}, u32[]{:S(2)}, u32[]{:S(2)}) collective-permute-start(f32[16,3072]{1,0:T(8,128)S(1)} %fusion), channel_id=1, source_target_pairs={{0,25},{1,26},{2,27},{3,28},{4,29},{5,30},{6,31},{7,32},{8,33},{9,... | collective-permute-start | bytes 589832
  550.2 37.6 %collective-permute-start.23 = (f32[16,3072]{1,0:T(8,128)S(1)}, f32[16,3072]{1,0:T(8,128)S(1)}, u32[]{:S(2)}, u32[]{:S(2)}) collective-permute-start(f32[16,3072]{1,0:T(8,128)S(1)} %fusion), channel_id=1, source_target_pairs={{0,24},{1,25},{2,26},{3,27},{4,28},{5,29},{6,30},{7,31},{8,32},{9,... | collective-permute-start | bytes 589832
  552.0 37.8 %collective-permute-start.22 = (f32[16,3072]{1,0:T(8,128)S(1)}, f32[16,3072]{1,0:T(8,128)S(1)}, u32[]{:S(2)}, u32[]{:S(2)}) collective-permute-start(f32[16,3072]{1,0:T(8,128)S(1)} %fusion), channel_id=1, source_target_pairs={{0,23},{1,24},{2,25},{3,26},{4,27},{5,28},{6,29},{7,30},{8,31},{9,... | collective-permute-start | bytes 589832
  567.3 28.4 %collective-permute-start.21 = (f32[16,3072]{1,0:T(8,128)S(1)}, f32[16,3072]{1,0:T(8,128)S(1)}, u32[]{:S(2)}, u32[]{:S(2)}) collective-permute-start(f32[16,3072]{1,0:T(8,128)S(1)} %fusion), channel_id=1, source_target_pairs={{0,22},{1,23},{2,24},{3,25},{4,26},{5,27},{6,28},{7,29},{8,30},{9,... | collective-permute-start | bytes 589832
  573.7 24.0 %collective-permute-start.20 = (f32[16,3072]{1,0:T(8,128)S(1)}, f32[16,3072]{1,0:T(8,128)S(1)}, u32[]{:S(2)}, u32[]{:S(2)}) collective-permute-start(f32[16,3072]{1,0:T(8,128)S(1)} %fusion), channel_id=1, source_target_pairs={{0,21},{1,22},{2,23},{3,24},{4,25},{5,26},{6,27},{7,28},{8,29},{9,... | collective-permute-start | bytes 589832
  579.4 23.7 %collective-permute-start.19 = (f32[16,3072]{1,0:T(8,128)S(1)}, f32[16,3072]{1,0:T(8,128)}, u32[]{:S(2)}, u32[]{:S(2)}) collective-permute-start(f32[16,3072]{1,0:T(8,128)S(1)} %fusion), channel_id=1, source_target_pairs={{0,20},{1,21},{2,22},{3,23},{4,24},{5,25},{6,26},{7,27},{8,28},{9,... | collective-permute-start | bytes 589832
  587.8 20.8 %collective-permute-start.18 = (f32[16,3072]{1,0:T(8,128)S(1)}, f32[16,3072]{1,0:T(8,128)}, u32[]{:S(2)}, u32[]{:S(2)}) collective-permute-start(f32[16,3072]{1,0:T(8,128)S(1)} %fusion), channel_id=1, source_target_pairs={{0,19},{1,20},{2,21},{3,22},{4,23},{5,24},{6,25},{7,26},{8,27},{9,... | collective-permute-start | bytes 589832
  589.8 31.1 %collective-permute-start.17 = (f32[16,3072]{1,0:T(8,128)S(1)}, f32[16,3072]{1,0:T(8,128)}, u32[]{:S(2)}, u32[]{:S(2)}) collective-permute-start(f32[16,3072]{1,0:T(8,128)S(1)} %fusion), channel_id=1, source_target_pairs={{0,18},{1,19},{2,20},{3,21},{4,22},{5,23},{6,24},{7,25},{8,26},{9,... | collective-permute-start | bytes 589832
  595.7 35.5 %collective-permute-start.16 = (f32[16,3072]{1,0:T(8,128)S(1)}, f32[16,3072]{1,0:T(8,128)}, u32[]{:S(2)}, u32[]{:S(2)}) collective-permute-start(f32[16,3072]{1,0:T(8,128)S(1)} %fusion), channel_id=1, source_target_pairs={{0,17},{1,18},{2,19},{3,20},{4,21},{5,22},{6,23},{7,24},{8,25},{9,... | collective-permute-start | bytes 589832
  597.7 48.2 %collective-permute-start.15 = (f32[16,3072]{1,0:T(8,128)S(1)}, f32[16,3072]{1,0:T(8,128)}, u32[]{:S(2)}, u32[]{:S(2)}) collective-permute-start(f32[16,3072]{1,0:T(8,128)S(1)} %fusion), channel_id=1, source_target_pairs={{0,16},{1,17},{2,18},{3,19},{4,20},{5,21},{6,22},{7,23},{8,24},{9,... | collective-permute-start | bytes 589832
  603.1 70.1 %collective-permute-start.14 = (f32[16,3072]{1,0:T(8,128)S(1)}, f32[16,3072]{1,0:T(8,128)S(1)}, u32[]{:S(2)}, u32[]{:S(2)}) collective-permute-start(f32[16,3072]{1,0:T(8,128)S(1)} %fusion), channel_id=1, source_target_pairs={{0,15},{1,16},{2,17},{3,18},{4,19},{5,20},{6,21},{7,22},{8,23},{9,... | collective-permute-start | bytes 589832
  608.6 65.9 %collective-permute-start.13 = (f32[16,3072]{1,0:T(8,128)S(1)}, f32[16,3072]{1,0:T(8,128)S(1)}, u32[]{:S(2)}, u32[]{:S(2)}) collective-permute-start(f32[16,3072]{1,0:T(8,128)S(1)} %fusion), channel_id=1, source_target_pairs={{0,14},{1,15},{2,16},{3,17},{4,18},{5,19},{6,20},{7,21},{8,22},{9,... | collective-permute-start | bytes 589832
  620.9 58.9 %collective-permute-start.12 = (f32[16,3072]{1,0:T(8,128)S(1)}, f32[16,3072]{1,0:T(8,128)S(1)}, u32[]{:S(2)}, u32[]{:S(2)}) collective-permute-start(f32[16,3072]{1,0:T(8,128)S(1)} %fusion), channel_id=1, source_target_pairs={{0,13},{1,14},{2,15},{3,16},{4,17},{5,18},{6,19},{7,20},{8,21},{9,... | collective-permute-start | bytes 589832
  631.2 50.6 %collective-permute-start.11 = (f32[16,3072]{1,0:T(8,128)S(1)}, f32[16,3072]{1,0:T(8,128)S(1)}, u32[]{:S(2)}, u32[]{:S(2)}) collective-permute-start(f32[16,3072]{1,0:T(8,128)S(1)} %fusion), channel_id=1, source_target_pairs={{0,12},{1,13},{2,14},{3,15},{4,16},{5,17},{6,18},{7,19},{8,20},{9,... | collective-permute-start | bytes 589832
  646.0 38.4 %collective-permute-start.10 = (f32[16,3072]{1,0:T(8,128)S(1)}, f32[16,3072]{1,0:T(8,128)S(1)}, u32[]{:S(2)}, u32[]{:S(2)}) collective-permute-start(f32[16,3072]{1,0:T(8,128)S(1)} %fusion), channel_id=1, source_target_pairs={{0,11},{1,12},{2,13},{3,14},{4,15},{5,16},{6,17},{7,18},{8,19},{9,... | collective-permute-start | bytes 589832
  673.3 23.7 %collective-permute-start.9 = (f32[16,3072]{1,0:T(8,128)S(1)}, f32[16,3072]{1,0:T(8,128)S(1)}, u32[]{:S(2)}, u32[]{:S(2)}) collective-permute-start(f32[16,3072]{1,0:T(8,128)S(1)} %fusion), channel_id=1, source_target_pairs={{0,10},{1,11},{2,12},{3,13},{4,14},{5,15},{6,16},{7,17},{8,18},{9,... | collective-permute-start | bytes 589832
  674.6 29.1 %collective-permute-start.8 = (f32[16,3072]{1,0:T(8,128)S(1)}, f32[16,3072]{1,0:T(8,128)S(1)}, u32[]{:S(2)}, u32[]{:S(2)}) collective-permute-start(f32[16,3072]{1,0:T(8,128)S(1)} %fusion), channel_id=1, source_target_pairs={{0,9},{1,10},{2,11},{3,12},{4,13},{5,14},{6,15},{7,16},{8,17},{9,1... | collective-permute-start | bytes 589832
  679.9 25.8 %collective-permute-start.7 = (f32[16,3072]{1,0:T(8,128)S(1)}, f32[16,3072]{1,0:T(8,128)S(1)}, u32[]{:S(2)}, u32[]{:S(2)}) collective-permute-start(f32[16,3072]{1,0:T(8,128)S(1)} %fusion), channel_id=1, source_target_pairs={{0,8},{1,9},{2,10},{3,11},{4,12},{5,13},{6,14},{7,15},{8,16},{9,17... | collective-permute-start | bytes 589832
  681.8 28.5 %collective-permute-start.6 = (f32[16,3072]{1,0:T(8,128)S(1)}, f32[16,3072]{1,0:T(8,128)S(1)}, u32[]{:S(2)}, u32[]{:S(2)}) collective-permute-start(f32[16,3072]{1,0:T(8,128)S(1)} %fusion), channel_id=1, source_target_pairs={{0,7},{1,8},{2,9},{3,10},{4,11},{5,12},{6,13},{7,14},{8,15},{9,16}... | collective-permute-start | bytes 589832
  685.1 27.1 %collective-permute-start.5 = (f32[16,3072]{1,0:T(8,128)S(1)}, f32[16,3072]{1,0:T(8,128)S(1)}, u32[]{:S(2)}, u32[]{:S(2)}) collective-permute-start(f32[16,3072]{1,0:T(8,128)S(1)} %fusion), channel_id=1, source_target_pairs={{0,6},{1,7},{2,8},{3,9},{4,10},{5,11},{6,12},{7,13},{8,14},{9,15},... | collective-permute-start | bytes 589832
  697.0 25.4 %collective-permute-start.4 = (f32[16,3072]{1,0:T(8,128)S(1)}, f32[16,3072]{1,0:T(8,128)}, u32[]{:S(2)}, u32[]{:S(2)}) collective-permute-start(f32[16,3072]{1,0:T(8,128)S(1)} %fusion), channel_id=1, source_target_pairs={{0,5},{1,6},{2,7},{3,8},{4,9},{5,10},{6,11},{7,12},{8,13},{9,14},{... | collective-permute-start | bytes 589832
  703.7 18.6 %collective-permute-start.3 = (f32[16,3072]{1,0:T(8,128)S(1)}, f32[16,3072]{1,0:T(8,128)}, u32[]{:S(2)}, u32[]{:S(2)}) collective-permute-start(f32[16,3072]{1,0:T(8,128)S(1)} %fusion), channel_id=1, source_target_pairs={{0,4},{1,5},{2,6},{3,7},{4,8},{5,9},{6,10},{7,11},{8,12},{9,13},{1... | collective-permute-start | bytes 589832
  705.7 16.7 %collective-permute-start.2 = (f32[16,3072]{1,0:T(8,128)S(1)}, f32[16,3072]{1,0:T(8,128)}, u32[]{:S(2)}, u32[]{:S(2)}) collective-permute-start(f32[16,3072]{1,0:T(8,128)S(1)} %fusion), channel_id=1, source_target_pairs={{0,3},{1,4},{2,5},{3,6},{4,7},{5,8},{6,9},{7,10},{8,11},{9,12},{10... | collective-permute-start | bytes 589832
  710.3 12.1 %collective-permute-start.1 = (f32[16,3072]{1,0:T(8,128)S(1)}, f32[16,3072]{1,0:T(8,128)}, u32[]{:S(2)}, u32[]{:S(2)}) collective-permute-start(f32[16,3072]{1,0:T(8,128)S(1)} %fusion), channel_id=1, source_target_pairs={{0,2},{1,3},{2,4},{3,5},{4,6},{5,7},{6,8},{7,9},{8,10},{9,11},{10,... | collective-permute-start | bytes 589832
  712.9 9.5 %collective-permute-start = (f32[16,3072]{1,0:T(8,128)S(1)}, f32[16,3072]{1,0:T(8,128)}, u32[]{:S(2)}, u32[]{:S(2)}) collective-permute-start(f32[16,3072]{1,0:T(8,128)S(1)} %fusion), channel_id=1, source_target_pairs={{0,1},{1,2},{2,3},{3,4},{4,5},{5,6},{6,7},{7,8},{8,9},{9,10},{10,1... | collective-permute-start | bytes 589832
  722.3 187.8 %all-gather.6.cloned.1.call-start = ((), (), s32[]{:S(2)}) async-start(), calls=%async_computation.2 | async-start | bytes 3342336 | tf_op jit(solution)/shard_map/all_gather | solution.py:111
  (78 other events, 4013.2 us)
Sparse Core Ops, SparseCore 0:
  9.7 57.9 all-gather.3
  722.4 139.3 all-reduce.6
  864.2 45.8 all-gather.5
where the time goes:
time: 927 us; the launch traced here: 924 us
  blocking collectives  424 us (46%)
  other arithmetic  145 us (16%)
  starting transfers between devices  136 us (15%)
  local copies, waits for them, and re-layouts  128 us (14%)
  waiting for transfers between devices  38.2 us (4%)
  matrix products  35.9 us (4%)
  between operations  16.2 us (2%)
    unnamed x1, blocking collectives  360 us
    unnamed x32, starting transfers between devices  136 us
    unnamed x153, local copies, waits for them, and re-layouts  92.8 us
    reduce_sum x4, other arithmetic, block_pass(): kernel_terms.append(jnp.sum(grad_conv * window * same_seg, axis=(0, 1)))  88.1 us
    psum x1, blocking collectives, local(): kernel_total, gain_total = lax.psum((kernel_part, gain_part), ('dp', 'red'))  63.9 us
    another operation x2, other arithmetic  35.5 us
    all_gather x1, waiting for transfers between devices, local(): weights = lax.all_gather(w_in, 'red', axis=0, tiled=True)  23.9 us
  transfers between devices with their start and end apart: 35, of which 3 were waited for; matrix products, arithmetic and copies ran while one was open for 20% of the time, Pallas kernels for 0%

commit v1 on v0

--- a/solution.py
+++ b/solution.py
@@ -109,7 +109,7 @@
         tiled=True,
     )
     grad_weights = lax.all_gather(owned_rows, "dp", axis=0, tiled=True)
-    kernel_total, gain_total = lax.psum((kernel_part, gain_part), ("dp", "red"))
+    kernel_total, gain_total = lax.psum(lax.psum((kernel_part, gain_part), "red"), "dp")
     return (
         module_output,
         frame_gradient,

time: 927 us -> 974 us (1.051)
  waiting for transfers between devices: 38.2 us -> 81.4 us
  blocking collectives: 424 us -> 409 us
    psum x1 -> x2, waiting for transfers between devices: 0.01 us -> 55.8 us  [the longest x1 55.8 us: local(): lax.psum((kernel_part, gain_part), 'red')]
    psum x1 -> x2, blocking collectives: 63.9 us -> 48.8 us  [the longest x1 34.1 us: local(): lax.psum(lax.psum((kernel_part, gain_part), 'red'), 'dp')]
    all_gather x1, waiting for transfers between devices: 12.9 us -> 0.01 us  [local(): grad_weights = lax.all_gather(owned_rows, 'dp', axis=0, tiled=True)]
    unnamed x153 -> x177, local copies, waits for them, and re-layouts: 92.8 us -> 93.3 us
  transfers between devices with their start and end apart: 35 -> 36, of which waited for: 3 -> 3; matrix products, arithmetic and copies ran while one was open for 20% -> 20% of each run, Pallas kernels for 0% -> 0%
where the time goes in v1:
time: 974 us; the launch traced here: 963 us
  blocking collectives  409 us (42%)
  other arithmetic  147 us (15%)
  starting transfers between devices  139 us (14%)
  local copies, waits for them, and re-layouts  134 us (14%)
  waiting for transfers between devices  81.4 us (8%)
  matrix products  35.9 us (4%)
  between operations  16.4 us (2%)
    unnamed x1, blocking collectives  360 us
    unnamed x32, starting transfers between devices  139 us
    unnamed x177, local copies, waits for them, and re-layouts  93.3 us
    reduce_sum x4, other arithmetic, block_pass(): kernel_terms.append(jnp.sum(grad_conv * window * same_seg, axis=(0, 1)))  89.1 us
    psum x1, waiting for transfers between devices, local(): lax.psum((kernel_part, gain_part), 'red')  55.8 us
    another operation x2, other arithmetic  35.5 us
    psum x1, blocking collectives, local(): lax.psum(lax.psum((kernel_part, gain_part), 'red'), 'dp')  34.1 us
    all_gather x1, waiting for transfers between devices, local(): weights = lax.all_gather(w_in, 'red', axis=0, tiled=True)  23.9 us
  transfers between devices with their start and end apart: 36, of which 3 were waited for; matrix products, arithmetic and copies ran while one was open for 20% of the time, Pallas kernels for 0%

profile of v1, /device:TPU:1, one launch (start us, length us, event | category | flops | bytes accessed | tf_op | source)
XLA Modules:
  0.0 962.6 jit_solution(8370592546768447698)
XLA Ops:
  14.4 8.3 copy.13
  22.7 10.7 %reshape_reshape.3 = bf16[768,8,16,12]{0,3,2,1:T(8,128)(2,1)} reshape(bf16[16,48,1536]{1,0,2:T(8,128)(2,1)} %copy.13) | data formatting | bytes 4718592 | tf_op jit(solution)/shard_map/reshape;reshape | solution.py:101
  37.4 5.2 reshape.139
  43.8 23.9 %all-gather.4.cloned.1.call-done = bf16[1536,3072]{1,0:T(8,128)(2,1)} async-done(((bf16[192,3072]{1,0:T(8,128)(2,1)}), bf16[1536,3072]{1,0:T(8,128)(2,1)}) %all-gather.4.cloned.1.call-update) | async-done | bytes 9437200 | tf_op jit(solution)/shard_map/all_gather | solution.py:88
  67.7 10.8 %fusion.3 = f32[16,48,3072]{2,1,0:T(8,128)S(1)} fusion(bf16[16,48,1536]{2,1,0:T(8,128)(2,1)} %fusion.11, bf16[1536,3072]{1,0:T(8,128)(2,1)} %all-gather.4.cloned.1.call-done), kind=kOutput, calls=%fused_computation.62 | convolution fusion | flops 7247757312 | bytes 21233664 | tf_op jit(solution)/shard_map/dot_general | solution.py:23
  82.6 49.2 %multiply_reduce_fusion = (f32[1536]{0:T(1024)}, f32[1536]{0:T(1024)}, f32[1536]{0:T(1024)}, f32[1536]{0:T(1024)}, f32[1536]{0:T(1024)}, /*index=5*/f32[1536]{0:...) fusion(f32[16,48,1536]{2,1,0:T(8,128)S(1)} %multiply_multiply_f, ...), kind=kLoop, calls=%fused_computation.186 | loop fusion | flops 150981120 | bytes 16856064 | tf_op jit(solution)/shard_map/reduce_sum | solution.py:50
  132.0 28.6 %multiply_convert_fusion.1 = (bf16[16,48,1536]{2,1,0:T(8,128)(2,1)S(1)}, f32[16,48,1536]{2,1,0:T(8,128)}) fusion(f32[16,48,3072]{2,1,0:T(8,128)} %copy-done.2, f32[16,48]{1,0:T(8,128)S(1)} %get-tuple-element.106, f32[16,48]{1,0:T(8,128)S(1)} %get-tuple-element.76, f32[1536]{0:T(1024)} %copy-done.68, f32[16,48]{1,0:T(8,128)S(1)} %get-tuple-element.77, ...), kind=kLoop, calls=%fused_computation.218 | loop fusion | flops 114425856 | bytes 16800768 | tf_op jit(solution)/shard_map/convert.4
  160.6 6.9 multiply_convert_fusion
  168.9 10.8 %fusion.119 = f32[1536,3072]{1,0:T(8,128)} fusion(bf16[768,1536]{0,1:T(8,128)(2,1)S(1)} %copy-done.7, bf16[768,1536]{1,0:T(8,128)(2,1)S(1)} %bitcast.26, bf16[768,1536]{1,0:T(8,128)(2,1)S(1)} %bitcast.25), kind=kOutput, calls=%fused_computation.182 | convolution fusion | flops 7257194496 | bytes 25952256 | tf_op jit(solution)/shard_map/dot_general | solution.py:104
  179.8 359.8 %fusion = f32[16,3072]{1,0:T(8,128)S(1)} fusion(f32[1536,3072]{1,0:T(8,128)} %fusion.119), kind=kCustom, calls=%all-reduce-scatter | all-reduce-scatter fusion | flops 6291457 | bytes 19070976
  552.7 15.0 %collective-permute-start.22 = (f32[16,3072]{1,0:T(8,128)S(1)}, f32[16,3072]{1,0:T(8,128)S(1)}, u32[]{:S(2)}, u32[]{:S(2)}) collective-permute-start(f32[16,3072]{1,0:T(8,128)S(1)} %fusion), channel_id=1, source_target_pairs={{0,23},{1,24},{2,25},{3,26},{4,27},{5,28},{6,29},{7,30},{8,31},{9,... | collective-permute-start | bytes 589832
  567.7 6.4 collective-permute-start.21
  574.1 5.7 collective-permute-start.20
  579.8 7.7 collective-permute-start.19
  588.9 6.6 collective-permute-start.17
  596.9 4.3 collective-permute-start.15
  601.2 5.9 collective-permute-start.14
  607.1 12.3 %collective-permute-start.13 = (f32[16,3072]{1,0:T(8,128)S(1)}, f32[16,3072]{1,0:T(8,128)S(1)}, u32[]{:S(2)}, u32[]{:S(2)}) collective-permute-start(f32[16,3072]{1,0:T(8,128)S(1)} %fusion), channel_id=1, source_target_pairs={{0,14},{1,15},{2,16},{3,17},{4,18},{5,19},{6,20},{7,21},{8,22},{9,... | collective-permute-start | bytes 589832
  619.4 10.3 %collective-permute-start.12 = (f32[16,3072]{1,0:T(8,128)S(1)}, f32[16,3072]{1,0:T(8,128)S(1)}, u32[]{:S(2)}, u32[]{:S(2)}) collective-permute-start(f32[16,3072]{1,0:T(8,128)S(1)} %fusion), channel_id=1, source_target_pairs={{0,13},{1,14},{2,15},{3,16},{4,17},{5,18},{6,19},{7,20},{8,21},{9,... | collective-permute-start | bytes 589832
  629.8 14.7 %collective-permute-start.11 = (f32[16,3072]{1,0:T(8,128)S(1)}, f32[16,3072]{1,0:T(8,128)S(1)}, u32[]{:S(2)}, u32[]{:S(2)}) collective-permute-start(f32[16,3072]{1,0:T(8,128)S(1)} %fusion), channel_id=1, source_target_pairs={{0,12},{1,13},{2,14},{3,15},{4,16},{5,17},{6,18},{7,19},{8,20},{9,... | collective-permute-start | bytes 589832
  646.7 26.1 %multiply_reduce_fusion.9 = (f32[1536]{0:T(1024)S(1)}, f32[1536]{0:T(1024)S(1)}, f32[1536]{0:T(1024)S(1)}, f32[1536]{0:T(1024)S(1)}, f32[1536]{0:T(1024)S(1)}, /...) fusion(f32[16,48,1536]{2,1,0:T(8,128)} %copy-done.1, f32[16,48,1536]{2,1,0:T(8,128)} %copy-done, ...), kind=kLoop, calls=%fused_computation.195 | loop fusion | flops 30657024 | bytes 9517056 | tf_op jit(solution)/shard_map/reduce_sum | solution.py:50
  674.3 5.2 collective-permute-start.8
  688.2 9.8 %multiply_reduce_fusion.18 = (f32[1536]{0:T(1024)S(1)}, f32[1536]{0:T(1024)S(1)}, f32[1536]{0:T(1024)S(1)}, f32[1536]{0:T(1024)S(1)}, f32[1536]{0:T(1024)S(1)}, ...) fusion(f32[16,48,1536]{2,1,0:T(8,128)} %copy-done.1, ...), kind=kLoop, calls=%fused_computation.204 | loop fusion | flops 31836672 | bytes 9520128 | tf_op jit(solution)/shard_map/reduce_sum | solution.py:50
  698.2 5.9 collective-permute-start.4
  706.1 6.9 collective-permute-start.2
  727.3 4.2 stack.127
  733.7 55.8 %all-reduce.8.cloned.1.call-done = f32[31,1536]{1,0:T(8,128)} async-done(((f32[31,1536]{1,0:T(8,128)}), f32[31,1536]{1,0:T(8,128)}) %all-reduce.8.cloned.1.call-update) | async-done | bytes 190480 | tf_op jit(solution)/shard_map/psum | solution.py:112
  789.6 84.6 %concatenate.17 = f32[524,3072]{1,0:T(8,128)} concatenate(f32[12,3072]{1,0:T(8,128)S(1)} %collective-permute-done.31, f32[16,3072]{1,0:T(8,128)S(1)} %collective-permute-done.30, f32[16,3072]{1,0:T(8,128)S(1)} %collective-permute-done.29, f32[16,3072]{1,0:T(8,128)S(1)} %copy-done.9, f32[16,3072]{1,0:T(8,128)} %copy-done.10, f32[16,3072]{1,0:T(8,128)} %copy-done.11, ...), dimensions={0} | concatenate | bytes 12877824
  876.0 14.3 %fusion.18 = (f32[1536]{0:T(1024)S(1)}, f32[16,48]{1,0:T(8,128)S(1)}, f32[16,48]{1,0:T(8,128)S(1)}, f32[16,48,1536]{2,1,0:T(8,128)}) fusion(bf16[16,48,1536]{2,1,0:T(8,128)(2,1)S(1)} %copy-done.3, f32[16,48]{1,0:T(8,128)S(1)} %copy-done.71, f32[16,48]{1,0:T(8,128)S(1)} %copy-done.63, f32[1536]{0:T(1024)S(1)} %copy-done.73, ...), kind=kOutput, calls=%fused_computation.80 | convolution fusion | flops 7267808256 | bytes 21258240 | tf_op jit(solution)/shard_map/dot_general | solution.py:67
  890.3 14.7 %psum.30 = f32[1536]{0:T(1024)S(1)} all-reduce(f32[1536]{0:T(1024)S(1)} %get-tuple-element.36), channel_id=1, replica_groups=mesh['dp'=16,'red'=8] {'red'}, use_global_device_ids=true, to_apply=%region_40.41 | all-reduce | flops 1536 | bytes 12288 | tf_op jit(solution)/shard_map/psum | solution.py:112
  905.0 34.1 %psum.31 = f32[1536]{0:T(1024)S(1)} all-reduce(f32[1536]{0:T(1024)S(1)} %psum.30), channel_id=1, replica_groups=mesh['dp'=16,'red'=8] {'dp'}, use_global_device_ids=true, to_apply=%region_41.42 | all-reduce | flops 1536 | bytes 12288 | tf_op jit(solution)/shard_map/psum | solution.py:112
  939.7 7.8 fusion.17
  (293 shorter events, 73.5 us)
Async XLA Ops:
  7.2 60.5 %all-gather.4.cloned.1.call-start = ((), (), s32[]{:S(2)}) async-start(), calls=%async_computation | async-start | bytes 10616832 | tf_op jit(solution)/shard_map/all_gather | solution.py:88
  7.9 781.5 %all-reduce.8.cloned.1.call-start = ((), (), s32[]{:S(2)}) async-start(), calls=%async_computation.1 | async-start | bytes 393216 | tf_op jit(solution)/shard_map/psum | solution.py:112
  539.7 8.2 collective-permute-start.30
  546.6 21.1 %collective-permute-start.26 = (f32[16,3072]{1,0:T(8,128)S(1)}, f32[16,3072]{1,0:T(8,128)S(1)}, u32[]{:S(2)}, u32[]{:S(2)}) collective-permute-start(f32[16,3072]{1,0:T(8,128)S(1)} %fusion), channel_id=1, source_target_pairs={{0,27},{1,28},{2,29},{3,30},{4,31},{5,32},{6,33},{7,34},{8,35},{9,... | collective-permute-start | bytes 589832
  547.9 26.2 %collective-permute-start.25 = (f32[16,3072]{1,0:T(8,128)S(1)}, f32[16,3072]{1,0:T(8,128)S(1)}, u32[]{:S(2)}, u32[]{:S(2)}) collective-permute-start(f32[16,3072]{1,0:T(8,128)S(1)} %fusion), channel_id=1, source_target_pairs={{0,26},{1,27},{2,28},{3,29},{4,30},{5,31},{6,32},{7,33},{8,34},{9,... | collective-permute-start | bytes 589832
  549.2 30.6 %collective-permute-start.24 = (f32[16,3072]{1,0:T(8,128)S(1)}, f32[16,3072]{1,0:T(8,128)S(1)}, u32[]{:S(2)}, u32[]{:S(2)}) collective-permute-start(f32[16,3072]{1,0:T(8,128)S(1)} %fusion), channel_id=1, source_target_pairs={{0,25},{1,26},{2,27},{3,28},{4,29},{5,30},{6,31},{7,32},{8,33},{9,... | collective-permute-start | bytes 589832
  550.5 37.0 %collective-permute-start.23 = (f32[16,3072]{1,0:T(8,128)S(1)}, f32[16,3072]{1,0:T(8,128)S(1)}, u32[]{:S(2)}, u32[]{:S(2)}) collective-permute-start(f32[16,3072]{1,0:T(8,128)S(1)} %fusion), channel_id=1, source_target_pairs={{0,24},{1,25},{2,26},{3,27},{4,28},{5,29},{6,30},{7,31},{8,32},{9,... | collective-permute-start | bytes 589832
  552.7 36.1 %collective-permute-start.22 = (f32[16,3072]{1,0:T(8,128)S(1)}, f32[16,3072]{1,0:T(8,128)S(1)}, u32[]{:S(2)}, u32[]{:S(2)}) collective-permute-start(f32[16,3072]{1,0:T(8,128)S(1)} %fusion), channel_id=1, source_target_pairs={{0,23},{1,24},{2,25},{3,26},{4,27},{5,28},{6,29},{7,30},{8,31},{9,... | collective-permute-start | bytes 589832
  567.7 27.8 %collective-permute-start.21 = (f32[16,3072]{1,0:T(8,128)S(1)}, f32[16,3072]{1,0:T(8,128)S(1)}, u32[]{:S(2)}, u32[]{:S(2)}) collective-permute-start(f32[16,3072]{1,0:T(8,128)S(1)} %fusion), channel_id=1, source_target_pairs={{0,22},{1,23},{2,24},{3,25},{4,26},{5,27},{6,28},{7,29},{8,30},{9,... | collective-permute-start | bytes 589832
  574.1 22.8 %collective-permute-start.20 = (f32[16,3072]{1,0:T(8,128)S(1)}, f32[16,3072]{1,0:T(8,128)S(1)}, u32[]{:S(2)}, u32[]{:S(2)}) collective-permute-start(f32[16,3072]{1,0:T(8,128)S(1)} %fusion), channel_id=1, source_target_pairs={{0,21},{1,22},{2,23},{3,24},{4,25},{5,26},{6,27},{7,28},{8,29},{9,... | collective-permute-start | bytes 589832
  579.8 21.4 %collective-permute-start.19 = (f32[16,3072]{1,0:T(8,128)S(1)}, f32[16,3072]{1,0:T(8,128)S(1)}, u32[]{:S(2)}, u32[]{:S(2)}) collective-permute-start(f32[16,3072]{1,0:T(8,128)S(1)} %fusion), channel_id=1, source_target_pairs={{0,20},{1,21},{2,22},{3,23},{4,24},{5,25},{6,26},{7,27},{8,28},{9,... | collective-permute-start | bytes 589832
  587.6 19.6 %collective-permute-start.18 = (f32[16,3072]{1,0:T(8,128)S(1)}, f32[16,3072]{1,0:T(8,128)S(1)}, u32[]{:S(2)}, u32[]{:S(2)}) collective-permute-start(f32[16,3072]{1,0:T(8,128)S(1)} %fusion), channel_id=1, source_target_pairs={{0,19},{1,20},{2,21},{3,22},{4,23},{5,24},{6,25},{7,26},{8,27},{9,... | collective-permute-start | bytes 589832
  588.9 30.5 %collective-permute-start.17 = (f32[16,3072]{1,0:T(8,128)S(1)}, f32[16,3072]{1,0:T(8,128)S(1)}, u32[]{:S(2)}, u32[]{:S(2)}) collective-permute-start(f32[16,3072]{1,0:T(8,128)S(1)} %fusion), channel_id=1, source_target_pairs={{0,18},{1,19},{2,20},{3,21},{4,22},{5,23},{6,24},{7,25},{8,26},{9,... | collective-permute-start | bytes 589832
  595.6 34.2 %collective-permute-start.16 = (f32[16,3072]{1,0:T(8,128)S(1)}, f32[16,3072]{1,0:T(8,128)S(1)}, u32[]{:S(2)}, u32[]{:S(2)}) collective-permute-start(f32[16,3072]{1,0:T(8,128)S(1)} %fusion), channel_id=1, source_target_pairs={{0,17},{1,18},{2,19},{3,20},{4,21},{5,22},{6,23},{7,24},{8,25},{9,... | collective-permute-start | bytes 589832
  596.9 47.6 %collective-permute-start.15 = (f32[16,3072]{1,0:T(8,128)S(1)}, f32[16,3072]{1,0:T(8,128)S(1)}, u32[]{:S(2)}, u32[]{:S(2)}) collective-permute-start(f32[16,3072]{1,0:T(8,128)S(1)} %fusion), channel_id=1, source_target_pairs={{0,16},{1,17},{2,18},{3,19},{4,20},{5,21},{6,22},{7,23},{8,24},{9,... | collective-permute-start | bytes 589832
  601.2 71.5 %collective-permute-start.14 = (f32[16,3072]{1,0:T(8,128)S(1)}, f32[16,3072]{1,0:T(8,128)S(1)}, u32[]{:S(2)}, u32[]{:S(2)}) collective-permute-start(f32[16,3072]{1,0:T(8,128)S(1)} %fusion), channel_id=1, source_target_pairs={{0,15},{1,16},{2,17},{3,18},{4,19},{5,20},{6,21},{7,22},{8,23},{9,... | collective-permute-start | bytes 589832
  607.1 67.1 %collective-permute-start.13 = (f32[16,3072]{1,0:T(8,128)S(1)}, f32[16,3072]{1,0:T(8,128)S(1)}, u32[]{:S(2)}, u32[]{:S(2)}) collective-permute-start(f32[16,3072]{1,0:T(8,128)S(1)} %fusion), channel_id=1, source_target_pairs={{0,14},{1,15},{2,16},{3,17},{4,18},{5,19},{6,20},{7,21},{8,22},{9,... | collective-permute-start | bytes 589832
  619.4 60.1 %collective-permute-start.12 = (f32[16,3072]{1,0:T(8,128)S(1)}, f32[16,3072]{1,0:T(8,128)S(1)}, u32[]{:S(2)}, u32[]{:S(2)}) collective-permute-start(f32[16,3072]{1,0:T(8,128)S(1)} %fusion), channel_id=1, source_target_pairs={{0,13},{1,14},{2,15},{3,16},{4,17},{5,18},{6,19},{7,20},{8,21},{9,... | collective-permute-start | bytes 589832
  629.8 51.7 %collective-permute-start.11 = (f32[16,3072]{1,0:T(8,128)S(1)}, f32[16,3072]{1,0:T(8,128)S(1)}, u32[]{:S(2)}, u32[]{:S(2)}) collective-permute-start(f32[16,3072]{1,0:T(8,128)S(1)} %fusion), channel_id=1, source_target_pairs={{0,12},{1,13},{2,14},{3,15},{4,16},{5,17},{6,18},{7,19},{8,20},{9,... | collective-permute-start | bytes 589832
  645.3 38.7 %collective-permute-start.10 = (f32[16,3072]{1,0:T(8,128)S(1)}, f32[16,3072]{1,0:T(8,128)S(1)}, u32[]{:S(2)}, u32[]{:S(2)}) collective-permute-start(f32[16,3072]{1,0:T(8,128)S(1)} %fusion), channel_id=1, source_target_pairs={{0,11},{1,12},{2,13},{3,14},{4,15},{5,16},{6,17},{7,18},{8,19},{9,... | collective-permute-start | bytes 589832
  672.8 25.4 %collective-permute-start.9 = (f32[16,3072]{1,0:T(8,128)S(1)}, f32[16,3072]{1,0:T(8,128)S(1)}, u32[]{:S(2)}, u32[]{:S(2)}) collective-permute-start(f32[16,3072]{1,0:T(8,128)S(1)} %fusion), channel_id=1, source_target_pairs={{0,10},{1,11},{2,12},{3,13},{4,14},{5,15},{6,16},{7,17},{8,18},{9,... | collective-permute-start | bytes 589832
  674.3 29.9 %collective-permute-start.8 = (f32[16,3072]{1,0:T(8,128)S(1)}, f32[16,3072]{1,0:T(8,128)S(1)}, u32[]{:S(2)}, u32[]{:S(2)}) collective-permute-start(f32[16,3072]{1,0:T(8,128)S(1)} %fusion), channel_id=1, source_target_pairs={{0,9},{1,10},{2,11},{3,12},{4,13},{5,14},{6,15},{7,16},{8,17},{9,1... | collective-permute-start | bytes 589832
  679.5 26.6 %collective-permute-start.7 = (f32[16,3072]{1,0:T(8,128)S(1)}, f32[16,3072]{1,0:T(8,128)S(1)}, u32[]{:S(2)}, u32[]{:S(2)}) collective-permute-start(f32[16,3072]{1,0:T(8,128)S(1)} %fusion), channel_id=1, source_target_pairs={{0,8},{1,9},{2,10},{3,11},{4,12},{5,13},{6,14},{7,15},{8,16},{9,17... | collective-permute-start | bytes 589832
  681.5 31.6 %collective-permute-start.6 = (f32[16,3072]{1,0:T(8,128)S(1)}, f32[16,3072]{1,0:T(8,128)S(1)}, u32[]{:S(2)}, u32[]{:S(2)}) collective-permute-start(f32[16,3072]{1,0:T(8,128)S(1)} %fusion), channel_id=1, source_target_pairs={{0,7},{1,8},{2,9},{3,10},{4,11},{5,12},{6,13},{7,14},{8,15},{9,16}... | collective-permute-start | bytes 589832
  684.7 30.6 %collective-permute-start.5 = (f32[16,3072]{1,0:T(8,128)S(1)}, f32[16,3072]{1,0:T(8,128)S(1)}, u32[]{:S(2)}, u32[]{:S(2)}) collective-permute-start(f32[16,3072]{1,0:T(8,128)S(1)} %fusion), channel_id=1, source_target_pairs={{0,6},{1,7},{2,8},{3,9},{4,10},{5,11},{6,12},{7,13},{8,14},{9,15},... | collective-permute-start | bytes 589832
  698.2 91.4 %collective-permute-start.4 = (f32[16,3072]{1,0:T(8,128)S(1)}, f32[16,3072]{1,0:T(8,128)}, u32[]{:S(2)}, u32[]{:S(2)}) collective-permute-start(f32[16,3072]{1,0:T(8,128)S(1)} %fusion), channel_id=1, source_target_pairs={{0,5},{1,6},{2,7},{3,8},{4,9},{5,10},{6,11},{7,12},{8,13},{9,14},{... | collective-permute-start | bytes 589832
  704.1 85.4 %collective-permute-start.3 = (f32[16,3072]{1,0:T(8,128)S(1)}, f32[16,3072]{1,0:T(8,128)}, u32[]{:S(2)}, u32[]{:S(2)}) collective-permute-start(f32[16,3072]{1,0:T(8,128)S(1)} %fusion), channel_id=1, source_target_pairs={{0,4},{1,5},{2,6},{3,7},{4,8},{5,9},{6,10},{7,11},{8,12},{9,13},{1... | collective-permute-start | bytes 589832
  706.1 83.5 %collective-permute-start.2 = (f32[16,3072]{1,0:T(8,128)S(1)}, f32[16,3072]{1,0:T(8,128)}, u32[]{:S(2)}, u32[]{:S(2)}) collective-permute-start(f32[16,3072]{1,0:T(8,128)S(1)} %fusion), channel_id=1, source_target_pairs={{0,3},{1,4},{2,5},{3,6},{4,7},{5,8},{6,9},{7,10},{8,11},{9,12},{10... | collective-permute-start | bytes 589832
  713.1 76.5 %collective-permute-start.1 = (f32[16,3072]{1,0:T(8,128)S(1)}, f32[16,3072]{1,0:T(8,128)}, u32[]{:S(2)}, u32[]{:S(2)}) collective-permute-start(f32[16,3072]{1,0:T(8,128)S(1)} %fusion), channel_id=1, source_target_pairs={{0,2},{1,3},{2,4},{3,5},{4,6},{5,7},{6,8},{7,9},{8,10},{9,11},{10,... | collective-permute-start | bytes 589832
  716.0 73.6 %collective-permute-start = (f32[16,3072]{1,0:T(8,128)S(1)}, f32[16,3072]{1,0:T(8,128)}, u32[]{:S(2)}, u32[]{:S(2)}) collective-permute-start(f32[16,3072]{1,0:T(8,128)S(1)} %fusion), channel_id=1, source_target_pairs={{0,1},{1,2},{2,3},{3,4},{4,5},{5,6},{6,7},{7,8},{8,9},{9,10},{10,1... | collective-permute-start | bytes 589832
  731.5 216.0 %all-reduce.10.cloned.1.call-start = ((), (), s32[]{:S(2)}) async-start(), calls=%async_computation.2 | async-start | bytes 393216 | tf_op jit(solution)/shard_map/psum | solution.py:112
  789.5 159.6 %all-gather.6.cloned.1.call-start = ((), (), s32[]{:S(2)}) async-start(), calls=%async_computation.3 | async-start | bytes 3342336 | tf_op jit(solution)/shard_map/all_gather | solution.py:111
  (91 other events, 7949.7 us)
Sparse Core Ops, SparseCore 0:
  9.7 57.9 all-gather.3
  731.7 57.7 all-reduce.7
  793.0 82.9 all-reduce.9
  878.3 48.5 all-gather.5
